TPU v7x, 128 devices: a whole 4x4x4 slice. The times are simulated.
128 devices in a mesh: section: 4 (over y), tensor: 32 (over z, x, core).
Axes of the slice: x: 4, y: 4, z: 4, core: 2. Of those that a mesh axis runs over, the one named last changes fastest.
Arguments:
- token_ids: int32 [4, 128], replicated, may hold values from 0 to 64127
- embedding: bfloat16 [64128, 8192], P('section', 'tensor'), may hold values from -6 to 6
- norm_gain: float32 [4, 8192], P('section'), may hold values from 0.1 to 1.9
- query_weight: bfloat16 [4, 8192, 8192], P('section', None, 'tensor'), may hold values from -0.0625 to 0.0625
- keyval_weight: bfloat16 [4, 8192, 2048], P('section', None, 'tensor'), may hold values from -0.0625 to 0.0625
- output_weight: bfloat16 [4, 8192, 8192], P('section', 'tensor'), may hold values from -0.0625 to 0.0625
- prefix_cache: bfloat16 [4, 128, 128, 2, 1024], P('section', 'tensor')
- prefix_lengths: int32 [128], P('tensor'), may hold values from 16 to 128, as said below
Outputs:
- answers: float32 [4, 128, 8192], P('section', 'tensor')
Inputs may be any that keep to these rules, and one draw needn't show every extreme that they name: `prefix_lengths`: some row has exactly 128 live positions.
All inputs are finite; a program needn't handle non-finite values.
Results may differ from a plain program's by a relative error of at most 0.039.
Values may be sent and summed in bfloat16 or wider, within the bound.
No kernel may reach another device: no remote copies, remote signals or barrier semaphores. Data moves between devices by JAX's collectives and lax.ppermute only.
A program may use at most 128 MiB of HBM per device.

v0:
```python
import jax
import jax.numpy as jnp
from jax import lax
from jax.sharding import PartitionSpec as P

HEADS = 64
KVH = 8
HD = 128
NORM_EPSILON = 1e-05
ROPE_BASE = 500000.0


def passed_along(block, axis, distance):
    devices = range(lax.axis_size(axis))
    route = [(i - distance, i) for i in devices if i - distance in devices]
    return lax.ppermute(block, axis, route)


def rope_tables(positions, head_dim):
    half_dim = head_dim // 2
    frequency = ROPE_BASE ** (-(jnp.arange(half_dim, dtype=jnp.float32) * 2.0 / head_dim))
    angles = positions.astype(jnp.float32)[:, None] * frequency[None, :]
    cosine = jnp.concatenate([jnp.cos(angles), jnp.cos(angles)], axis=-1)
    sine_table = jnp.concatenate([jnp.sin(angles), jnp.sin(angles)], axis=-1)
    return (cosine, sine_table)


def rotate(vectors, cosine, sine_table):
    half_dim = vectors.shape[-1] // 2
    swapped = jnp.concatenate([-vectors[..., half_dim:], vectors[..., :half_dim]], axis=-1)
    return vectors * cosine[:, None, :] + swapped * sine_table[:, None, :]


def normalize(values, gain_vec):
    scaling = lax.rsqrt(jnp.mean(values * values, axis=-1, keepdims=True) + NORM_EPSILON)
    return (values * scaling * gain_vec).astype(jnp.bfloat16)


def attend(queries, prefix, fresh_rows, live_len, step_index):
    row_count, kv_heads, group_size, head_dim = queries.shape
    step_total = fresh_rows.shape[0]
    past_keys = prefix[:, :, 0, :].reshape(row_count, -1, kv_heads, head_dim)
    past_vals = prefix[:, :, 1, :].reshape(row_count, -1, kv_heads, head_dim)
    new_keys = fresh_rows[:, :, 0, :].reshape(step_total, row_count, kv_heads, head_dim)
    new_vals = fresh_rows[:, :, 1, :].reshape(step_total, row_count, kv_heads, head_dim)
    score_scale = head_dim ** (-0.5)
    past_score = (
        jnp.einsum("rkgd,rlkd->rkgl", queries, past_keys, preferred_element_type=jnp.float32)
        * score_scale
    )
    new_score = (
        jnp.einsum("rkgd,srkd->rkgs", queries, new_keys, preferred_element_type=jnp.float32)
        * score_scale
    )
    past_mask = jnp.arange(past_keys.shape[1])[None, None, None, :] < live_len[:, None, None, None]
    new_mask = jnp.arange(step_total)[None, None, None, :] <= step_index
    past_score = jnp.where(past_mask, past_score, -1e30)
    new_score = jnp.where(new_mask, new_score, -1e30)
    top_score = jnp.maximum(jnp.max(past_score, axis=-1), jnp.max(new_score, axis=-1))[..., None]
    past_weight = jnp.exp(past_score - top_score)
    new_weight = jnp.exp(new_score - top_score)
    weight_total = jnp.sum(past_weight, axis=-1, keepdims=True) + jnp.sum(
        new_weight, axis=-1, keepdims=True
    )
    past_prob = (past_weight / weight_total).astype(jnp.bfloat16)
    new_prob = (new_weight / weight_total).astype(jnp.bfloat16)
    attended = jnp.einsum(
        "rkgl,rlkd->rkgd", past_prob, past_vals, preferred_element_type=jnp.float32
    )
    attended = attended + jnp.einsum(
        "rkgs,srkd->rkgd", new_prob, new_vals, preferred_element_type=jnp.float32
    )
    return attended.astype(jnp.bfloat16).reshape(row_count, kv_heads * group_size * head_dim)


def body(
    token_ids,
    embedding,
    norm_gain,
    query_weight,
    keyval_weight,
    output_weight,
    prefix_cache,
    prefix_lengths,
):
    n_tensor = lax.axis_size("tensor")
    section_pos = lax.axis_index("section")
    tensor_pos = lax.axis_index("tensor")
    last_section = lax.axis_size("section") - 1
    step_count = token_ids.shape[0]
    vocab_part = embedding.shape[0]
    own_rows = prefix_lengths.shape[0]
    model_width = embedding.shape[1] * n_tensor
    kv_width = KVH * HD
    group_size = HEADS // KVH
    local_ids = token_ids - section_pos * vocab_part
    inside = (local_ids >= 0) & (local_ids < vocab_part)
    picked = jnp.take(embedding, jnp.clip(local_ids, 0, vocab_part - 1), axis=0)
    partial_embed = jnp.where(inside[:, :, None], picked.astype(jnp.float32), 0.0)
    columns = lax.psum(partial_embed.astype(jnp.bfloat16), "section")
    own_embed = lax.all_to_all(columns, "tensor", split_axis=1, concat_axis=2, tiled=True)
    block_count = 1
    block_rows = own_rows // block_count
    item_count = step_count * block_count
    tick_count = item_count + last_section
    gain_vec = norm_gain[0]
    query_mat = query_weight[0]
    keyval_mat = keyval_weight[0]
    output_mat = output_weight[0]
    cache_rows = prefix_cache[0]
    carried = jnp.zeros((block_rows, model_width), jnp.float32)
    fresh_kv = jnp.zeros((step_count, own_rows, 2, kv_width), jnp.bfloat16)
    finals = jnp.zeros((step_count, own_rows, model_width), jnp.float32)

    def advance(tick_index, carry_state):
        incoming, fresh_kv, finals = carry_state
        item_index = tick_index - section_pos
        is_valid = (item_index >= 0) & (item_index < item_count)
        item_index = jnp.clip(item_index, 0, item_count - 1)
        step_index = item_index // block_count
        row_start = item_index % block_count * block_rows
        step_embed = lax.dynamic_index_in_dim(own_embed, step_index, 0, keepdims=False)
        first_input = step_embed.astype(jnp.float32)
        hidden_in = jnp.where(section_pos == 0, first_input, incoming)
        normed = lax.all_gather(normalize(hidden_in, gain_vec), "tensor", axis=0, tiled=True)
        queries = jnp.dot(normed, query_mat, preferred_element_type=jnp.float32)
        keyvals = jnp.dot(normed, keyval_mat, preferred_element_type=jnp.float32)
        queries, keyvals = (
            lax.all_to_all(queries, "tensor", split_axis=0, concat_axis=1, tiled=True),
            lax.all_to_all(keyvals, "tensor", split_axis=0, concat_axis=1, tiled=True),
        )
        cosine, sine_table = rope_tables(prefix_lengths + step_index, HD)
        turned_q = rotate(queries.reshape(block_rows, HEADS, HD), cosine, sine_table).astype(
            jnp.bfloat16
        )
        turned_k = rotate(
            keyvals[:, :kv_width].reshape(block_rows, KVH, HD), cosine, sine_table
        ).astype(jnp.bfloat16)
        value_cols = keyvals[:, kv_width:].astype(jnp.bfloat16)
        entry_kv = jnp.stack([turned_k.reshape(block_rows, kv_width), value_cols], axis=1)
        current = lax.dynamic_slice(
            fresh_kv, (step_index, row_start, 0, 0), (1, block_rows, 2, kv_width)
        )
        fresh_kv = lax.dynamic_update_slice(
            fresh_kv, jnp.where(is_valid, entry_kv[None], current), (step_index, row_start, 0, 0)
        )
        mixed_out = attend(
            turned_q.reshape(block_rows, KVH, group_size, HD),
            cache_rows,
            fresh_kv,
            prefix_lengths,
            step_index,
        )
        head_cols = lax.all_to_all(mixed_out, "tensor", split_axis=1, concat_axis=0, tiled=True)
        partial_value = (
            jnp.dot(head_cols, output_mat, preferred_element_type=jnp.float32)
            .astype(jnp.bfloat16)
            .astype(jnp.float32)
        )
        summed_all = lax.psum(partial_value.astype(jnp.bfloat16), "tensor").astype(jnp.float32)
        summed = lax.dynamic_slice_in_dim(summed_all, tensor_pos * block_rows, block_rows, 0)
        hidden_out = hidden_in + summed
        write_final = is_valid & (section_pos == last_section)
        current_final = lax.dynamic_slice(
            finals, (step_index, row_start, 0), (1, block_rows, model_width)
        )
        finals = lax.dynamic_update_slice(
            finals,
            jnp.where(write_final, hidden_out[None], current_final),
            (step_index, row_start, 0),
        )
        outgoing = passed_along(hidden_out, "section", 1)
        return (outgoing, fresh_kv, finals)

    spent, fresh_kv, finals = lax.fori_loop(0, tick_count, advance, (carried, fresh_kv, finals))
    answers = lax.psum_scatter(finals, "section", scatter_dimension=0, tiled=True)
    return answers


def solution(mesh):
    in_specs = (
        P(),
        P("section", "tensor"),
        P("section", None),
        P("section", None, "tensor"),
        P("section", None, "tensor"),
        P("section", "tensor", None),
        P("section", "tensor", None, None, None),
        P("tensor"),
    )
    out_specs = P("section", "tensor", None)
    return jax.shard_map(body, mesh=mesh, in_specs=in_specs, out_specs=out_specs, check_vma=False)
```

profile of v0, /device:TPU:0, one launch (start us, length us, event | category | flops | bytes accessed | tf_op | source)
XLA Modules:
  0.0 1589.0 jit_solution(3336385134684504714)
XLA Ops:
  8.2 5.9 gather_fusion
  15.2 44.3 %all-reduce.5.cloned.1.call-done = bf16[4,128,256]{2,0,1:T(4,128)(2,1)} async-done(((bf16[4,128,256]{2,0,1:T(4,128)(2,1)}), bf16[4,128,256]{2,0,1:T(4,128)(2,1)}) %all-reduce.5.cloned.1.call-update) | async-done | bytes 262160 | tf_op jit(solution)/shard_map/psum | solution.py:100
  59.5 7.2 all-to-all-start.3
  66.8 5.0 copy.62
  76.9 1456.6 %while.19 = (s32[]{:T(128)}, f32[4,8192]{1,0:T(4,128)S(1)}, bf16[4,4,2,1024]{3,1,2,0:T(4,128)(2,1)S(1)}, f32[4,4,8192]{2,1,0:T(4,128)}, pred[]{:T(512)}, /*index...) while((s32[]{:T(128)}, f32[4,8192]{1,0:T(4,128)S(1)}, ...), condition=%wide.region_8.9_spmd, body=%wide.region_1.8_spmd.sunk | while | flops 1228397952 | bytes 74761704 | solution.py:175
  81.3 41.5 %all-gather.5.cloned.1.call-done = bf16[32,4,8192]{2,1,0:T(4,128)(2,1)} async-done(((bf16[1,4,8192]{2,1,0:T(4,128)(2,1)}), bf16[32,4,8192]{2,1,0:T(4,128)(2,1)}) %all-gather.5.cloned.1.call-update) | async-done | bytes 2097168 | tf_op jit(solution)/shard_map/while/body/eval_jaxpr/all_gather | solution.py:125
  128.3 5.2 all-to-all-start.1
  147.3 5.3 all-to-all-done
  155.0 11.0 all_to_all.139
  166.0 4.3 convolution_convert_fusion.2
  170.3 105.2 %all-reduce.9.cloned.1.call-done = bf16[128,8192]{1,0:T(8,128)(2,1)} async-done(((bf16[128,8192]{1,0:T(8,128)(2,1)}), bf16[128,8192]{1,0:T(8,128)(2,1)}) %all-reduce.9.cloned.1.call-update) | async-done | bytes 2097168 | tf_op jit(solution)/shard_map/while/body/eval_jaxpr/psum | solution.py:160
  287.8 43.3 %all-gather.5.cloned.1.call-done = bf16[32,4,8192]{2,1,0:T(4,128)(2,1)} async-done(((bf16[1,4,8192]{2,1,0:T(4,128)(2,1)}), bf16[32,4,8192]{2,1,0:T(4,128)(2,1)}) %all-gather.5.cloned.1.call-update) | async-done | bytes 2097168 | tf_op jit(solution)/shard_map/while/body/eval_jaxpr/all_gather | solution.py:125
  336.7 5.2 all-to-all-start.1
  355.7 5.3 all-to-all-done
  363.3 11.0 all_to_all.139
  374.3 4.3 convolution_convert_fusion.2
  378.6 105.2 %all-reduce.9.cloned.1.call-done = bf16[128,8192]{1,0:T(8,128)(2,1)} async-done(((bf16[128,8192]{1,0:T(8,128)(2,1)}), bf16[128,8192]{1,0:T(8,128)(2,1)}) %all-reduce.9.cloned.1.call-update) | async-done | bytes 2097168 | tf_op jit(solution)/shard_map/while/body/eval_jaxpr/psum | solution.py:160
  496.1 43.3 %all-gather.5.cloned.1.call-done = bf16[32,4,8192]{2,1,0:T(4,128)(2,1)} async-done(((bf16[1,4,8192]{2,1,0:T(4,128)(2,1)}), bf16[32,4,8192]{2,1,0:T(4,128)(2,1)}) %all-gather.5.cloned.1.call-update) | async-done | bytes 2097168 | tf_op jit(solution)/shard_map/while/body/eval_jaxpr/all_gather | solution.py:125
  545.0 5.2 all-to-all-start.1
  564.0 5.3 all-to-all-done
  571.6 11.0 all_to_all.139
  582.6 4.3 convolution_convert_fusion.2
  586.9 105.2 %all-reduce.9.cloned.1.call-done = bf16[128,8192]{1,0:T(8,128)(2,1)} async-done(((bf16[128,8192]{1,0:T(8,128)(2,1)}), bf16[128,8192]{1,0:T(8,128)(2,1)}) %all-reduce.9.cloned.1.call-update) | async-done | bytes 2097168 | tf_op jit(solution)/shard_map/while/body/eval_jaxpr/psum | solution.py:160
  704.4 43.7 %all-gather.5.cloned.1.call-done = bf16[32,4,8192]{2,1,0:T(4,128)(2,1)} async-done(((bf16[1,4,8192]{2,1,0:T(4,128)(2,1)}), bf16[32,4,8192]{2,1,0:T(4,128)(2,1)}) %all-gather.5.cloned.1.call-update) | async-done | bytes 2097168 | tf_op jit(solution)/shard_map/while/body/eval_jaxpr/all_gather | solution.py:125
  753.6 5.2 all-to-all-start.1
  772.6 5.3 all-to-all-done
  780.2 11.0 all_to_all.139
  791.2 4.3 convolution_convert_fusion.2
  795.5 105.2 %all-reduce.9.cloned.1.call-done = bf16[128,8192]{1,0:T(8,128)(2,1)} async-done(((bf16[128,8192]{1,0:T(8,128)(2,1)}), bf16[128,8192]{1,0:T(8,128)(2,1)}) %all-reduce.9.cloned.1.call-update) | async-done | bytes 2097168 | tf_op jit(solution)/shard_map/while/body/eval_jaxpr/psum | solution.py:160
  913.0 43.4 %all-gather.5.cloned.1.call-done = bf16[32,4,8192]{2,1,0:T(4,128)(2,1)} async-done(((bf16[1,4,8192]{2,1,0:T(4,128)(2,1)}), bf16[32,4,8192]{2,1,0:T(4,128)(2,1)}) %all-gather.5.cloned.1.call-update) | async-done | bytes 2097168 | tf_op jit(solution)/shard_map/while/body/eval_jaxpr/all_gather | solution.py:125
  961.9 5.2 all-to-all-start.1
  980.9 5.3 all-to-all-done
  988.5 11.0 all_to_all.139
  999.5 4.3 convolution_convert_fusion.2
  1003.8 105.2 %all-reduce.9.cloned.1.call-done = bf16[128,8192]{1,0:T(8,128)(2,1)} async-done(((bf16[128,8192]{1,0:T(8,128)(2,1)}), bf16[128,8192]{1,0:T(8,128)(2,1)}) %all-reduce.9.cloned.1.call-update) | async-done | bytes 2097168 | tf_op jit(solution)/shard_map/while/body/eval_jaxpr/psum | solution.py:160
  1121.3 43.3 %all-gather.5.cloned.1.call-done = bf16[32,4,8192]{2,1,0:T(4,128)(2,1)} async-done(((bf16[1,4,8192]{2,1,0:T(4,128)(2,1)}), bf16[32,4,8192]{2,1,0:T(4,128)(2,1)}) %all-gather.5.cloned.1.call-update) | async-done | bytes 2097168 | tf_op jit(solution)/shard_map/while/body/eval_jaxpr/all_gather | solution.py:125
  1170.2 5.2 all-to-all-start.1
  1189.2 5.3 all-to-all-done
  1196.8 11.0 all_to_all.139
  1207.8 4.3 convolution_convert_fusion.2
  1212.1 105.2 %all-reduce.9.cloned.1.call-done = bf16[128,8192]{1,0:T(8,128)(2,1)} async-done(((bf16[128,8192]{1,0:T(8,128)(2,1)}), bf16[128,8192]{1,0:T(8,128)(2,1)}) %all-reduce.9.cloned.1.call-update) | async-done | bytes 2097168 | tf_op jit(solution)/shard_map/while/body/eval_jaxpr/psum | solution.py:160
  1329.6 43.3 %all-gather.5.cloned.1.call-done = bf16[32,4,8192]{2,1,0:T(4,128)(2,1)} async-done(((bf16[1,4,8192]{2,1,0:T(4,128)(2,1)}), bf16[32,4,8192]{2,1,0:T(4,128)(2,1)}) %all-gather.5.cloned.1.call-update) | async-done | bytes 2097168 | tf_op jit(solution)/shard_map/while/body/eval_jaxpr/all_gather | solution.py:125
  1378.5 5.2 all-to-all-start.1
  1397.5 5.3 all-to-all-done
  1405.1 11.0 all_to_all.139
  1416.1 4.3 convolution_convert_fusion.2
  1420.4 105.3 %all-reduce.9.cloned.1.call-done = bf16[128,8192]{1,0:T(8,128)(2,1)} async-done(((bf16[128,8192]{1,0:T(8,128)(2,1)}), bf16[128,8192]{1,0:T(8,128)(2,1)}) %all-reduce.9.cloned.1.call-update) | async-done | bytes 2097168 | tf_op jit(solution)/shard_map/while/body/eval_jaxpr/psum | solution.py:160
  1535.3 44.9 %all-reduce.7.cloned.1.call-done = f32[4,4,8192]{2,1,0:T(4,128)} async-done(((f32[4,4,8192]{2,1,0:T(4,128)}), f32[4,4,8192]{2,1,0:T(4,128)}) %all-reduce.7.cloned.1.call-update) | async-done | bytes 524304
  (571 shorter events, 246.9 us)
Async XLA Ops:
  6.5 53.0 %all-reduce.5.cloned.1.call-start = ((), (), s32[]{:S(2)}) async-start(), calls=%async_computation.4 | async-start | bytes 524288 | tf_op jit(solution)/shard_map/psum | solution.py:100
  59.5 16.1 %all-to-all-start.3 = ((bf16[4,128,256]{2,0,1:T(4,128)(2,1)}), bf16[4,128,256]{2,0,1:T(4,128)(2,1)S(1)}, u32[]{:S(2)}, u32[]{:S(2)}) async-start(bf16[4,128,256]{2,0,1:T(4,128)(2,1)} %all-reduce.5.cloned.1.call-done), calls=%async_computation.3 | async-start | bytes 524288 | tf_op jit(solution)/shard_map/all_to_all | solution.py:101
  76.9 45.9 %all-gather.5.cloned.1.call-start = ((), (), s32[]{:S(2)}) async-start(), calls=%async_computation.6 | async-start | bytes 2162688 | tf_op jit(solution)/shard_map/while/body/eval_jaxpr/all_gather | solution.py:125
  128.3 12.6 all-to-all-start.1
  141.0 11.7 all-to-all-start
  144.9 130.6 %all-reduce.9.cloned.1.call-start = ((), (), s32[]{:S(2)}) async-start(), calls=%async_computation.7 | async-start | bytes 4194304 | tf_op jit(solution)/shard_map/while/body/eval_jaxpr/psum | solution.py:160
  170.2 113.1 %copy-start.2 = (bf16[4,128,2,1024]{1,3,0,2:T(8,128)(2,1)S(1)}, bf16[4,128,2,1024]{1,3,0,2:T(8,128)(2,1)}, u32[]{:S(2)}) copy-start(bf16[4,128,2,1024]{1,3,0,2:T(8,128)(2,1)} %copy-done.1) | copy-start | bytes 6291460 | tf_op jit(solution)/shard_map/while
  170.2 113.1 %copy-start.4 = (bf16[4,4,8192]{2,1,0:T(4,128)(2,1)S(1)}, bf16[4,4,8192]{2,1,0:T(4,128)(2,1)}, u32[]{:S(2)}) copy-start(bf16[4,4,8192]{2,1,0:T(4,128)(2,1)} %copy-done.3) | copy-start | bytes 786436 | tf_op jit(solution)/shard_map/while
  170.2 113.1 %copy-start.12 = (s32[4]{0:T(128)S(1)}, s32[4]{0:T(128)}, u32[]{:S(2)}) copy-start(s32[4]{0:T(128)} %get-tuple-element.613) | copy-start | bytes 52 | tf_op jit(solution)/shard_map/while
  277.2 6.1 collective-permute-start
  283.4 47.8 %all-gather.5.cloned.1.call-start = ((), (), s32[]{:S(2)}) async-start(), calls=%async_computation.6 | async-start | bytes 2162688 | tf_op jit(solution)/shard_map/while/body/eval_jaxpr/all_gather | solution.py:125
  336.7 12.6 all-to-all-start.1
  349.3 11.7 all-to-all-start
  353.2 130.6 %all-reduce.9.cloned.1.call-start = ((), (), s32[]{:S(2)}) async-start(), calls=%async_computation.7 | async-start | bytes 4194304 | tf_op jit(solution)/shard_map/while/body/eval_jaxpr/psum | solution.py:160
  378.5 113.1 %copy-start.2 = (bf16[4,128,2,1024]{1,3,0,2:T(8,128)(2,1)S(1)}, bf16[4,128,2,1024]{1,3,0,2:T(8,128)(2,1)}, u32[]{:S(2)}) copy-start(bf16[4,128,2,1024]{1,3,0,2:T(8,128)(2,1)} %copy-done.1) | copy-start | bytes 6291460 | tf_op jit(solution)/shard_map/while
  378.5 113.1 %copy-start.4 = (bf16[4,4,8192]{2,1,0:T(4,128)(2,1)S(1)}, bf16[4,4,8192]{2,1,0:T(4,128)(2,1)}, u32[]{:S(2)}) copy-start(bf16[4,4,8192]{2,1,0:T(4,128)(2,1)} %copy-done.3) | copy-start | bytes 786436 | tf_op jit(solution)/shard_map/while
  378.5 113.1 %copy-start.12 = (s32[4]{0:T(128)S(1)}, s32[4]{0:T(128)}, u32[]{:S(2)}) copy-start(s32[4]{0:T(128)} %get-tuple-element.613) | copy-start | bytes 52 | tf_op jit(solution)/shard_map/while
  485.5 6.1 collective-permute-start
  491.7 47.8 %all-gather.5.cloned.1.call-start = ((), (), s32[]{:S(2)}) async-start(), calls=%async_computation.6 | async-start | bytes 2162688 | tf_op jit(solution)/shard_map/while/body/eval_jaxpr/all_gather | solution.py:125
  545.0 12.6 all-to-all-start.1
  557.6 11.7 all-to-all-start
  561.5 130.6 %all-reduce.9.cloned.1.call-start = ((), (), s32[]{:S(2)}) async-start(), calls=%async_computation.7 | async-start | bytes 4194304 | tf_op jit(solution)/shard_map/while/body/eval_jaxpr/psum | solution.py:160
  693.8 6.1 collective-permute-start
  700.0 48.1 %all-gather.5.cloned.1.call-start = ((), (), s32[]{:S(2)}) async-start(), calls=%async_computation.6 | async-start | bytes 2162688 | tf_op jit(solution)/shard_map/while/body/eval_jaxpr/all_gather | solution.py:125
  753.6 12.6 all-to-all-start.1
  766.2 11.7 all-to-all-start
  770.1 130.6 %all-reduce.9.cloned.1.call-start = ((), (), s32[]{:S(2)}) async-start(), calls=%async_computation.7 | async-start | bytes 4194304 | tf_op jit(solution)/shard_map/while/body/eval_jaxpr/psum | solution.py:160
  902.4 6.1 collective-permute-start
  908.6 47.8 %all-gather.5.cloned.1.call-start = ((), (), s32[]{:S(2)}) async-start(), calls=%async_computation.6 | async-start | bytes 2162688 | tf_op jit(solution)/shard_map/while/body/eval_jaxpr/all_gather | solution.py:125
  961.9 12.6 all-to-all-start.1
  974.5 11.7 all-to-all-start
  978.4 130.6 %all-reduce.9.cloned.1.call-start = ((), (), s32[]{:S(2)}) async-start(), calls=%async_computation.7 | async-start | bytes 4194304 | tf_op jit(solution)/shard_map/while/body/eval_jaxpr/psum | solution.py:160
  1003.8 113.1 %copy-start.12 = (s32[4]{0:T(128)S(1)}, s32[4]{0:T(128)}, u32[]{:S(2)}) copy-start(s32[4]{0:T(128)} %get-tuple-element.613) | copy-start | bytes 52 | tf_op jit(solution)/shard_map/while
  1110.7 6.1 collective-permute-start
  1116.9 47.8 %all-gather.5.cloned.1.call-start = ((), (), s32[]{:S(2)}) async-start(), calls=%async_computation.6 | async-start | bytes 2162688 | tf_op jit(solution)/shard_map/while/body/eval_jaxpr/all_gather | solution.py:125
  1170.2 12.6 all-to-all-start.1
  1182.8 11.7 all-to-all-start
  1186.7 130.6 %all-reduce.9.cloned.1.call-start = ((), (), s32[]{:S(2)}) async-start(), calls=%async_computation.7 | async-start | bytes 4194304 | tf_op jit(solution)/shard_map/while/body/eval_jaxpr/psum | solution.py:160
  1319.0 6.1 collective-permute-start
  1325.2 47.8 %all-gather.5.cloned.1.call-start = ((), (), s32[]{:S(2)}) async-start(), calls=%async_computation.6 | async-start | bytes 2162688 | tf_op jit(solution)/shard_map/while/body/eval_jaxpr/all_gather | solution.py:125
  1378.5 12.6 all-to-all-start.1
  1391.2 11.7 all-to-all-start
  1395.0 130.6 %all-reduce.9.cloned.1.call-start = ((), (), s32[]{:S(2)}) async-start(), calls=%async_computation.7 | async-start | bytes 4194304 | tf_op jit(solution)/shard_map/while/body/eval_jaxpr/psum | solution.py:160
  1420.4 113.1 %copy-start.2 = (bf16[4,128,2,1024]{1,3,0,2:T(8,128)(2,1)S(1)}, bf16[4,128,2,1024]{1,3,0,2:T(8,128)(2,1)}, u32[]{:S(2)}) copy-start(bf16[4,128,2,1024]{1,3,0,2:T(8,128)(2,1)} %copy-done.1) | copy-start | bytes 6291460 | tf_op jit(solution)/shard_map/while
  1420.4 113.1 %copy-start.4 = (bf16[4,4,8192]{2,1,0:T(4,128)(2,1)S(1)}, bf16[4,4,8192]{2,1,0:T(4,128)(2,1)}, u32[]{:S(2)}) copy-start(bf16[4,4,8192]{2,1,0:T(4,128)(2,1)} %copy-done.3) | copy-start | bytes 786436 | tf_op jit(solution)/shard_map/while
  1420.4 113.1 %copy-start.12 = (s32[4]{0:T(128)S(1)}, s32[4]{0:T(128)}, u32[]{:S(2)}) copy-start(s32[4]{0:T(128)} %get-tuple-element.613) | copy-start | bytes 52 | tf_op jit(solution)/shard_map/while
  1527.4 6.1 collective-permute-start
  1533.5 46.7 %all-reduce.7.cloned.1.call-start = ((), (), s32[]{:S(2)}) async-start(), calls=%async_computation.5 | async-start | bytes 1048576
  (70 other events, 1902.9 us)
Sparse Core Ops, SparseCore 0:
  15.4 44.1 all-reduce.4
  80.3 42.4 all-gather.4
  170.4 105.0 all-reduce.8
  286.4 44.6 all-gather.4
  378.7 105.0 all-reduce.8
  494.7 44.6 all-gather.4
  587.0 105.0 all-reduce.8
  703.3 44.6 all-gather.4
  795.6 105.0 all-reduce.8
  911.6 44.6 all-gather.4
  1003.9 105.0 all-reduce.8
  1119.9 44.6 all-gather.4
  1212.2 105.0 all-reduce.8
  1328.2 44.6 all-gather.4
  1420.5 105.0 all-reduce.8
  1536.5 43.7 all-reduce.6
where the time goes:
time: 1590 us
  waiting for transfers between devices  1210 us (76%)
  starting transfers between devices  95.2 us (6%)
  matrix products  77.1 us (5%)
  blocking collectives  76.7 us (5%)
  local copies, waits for them, and re-layouts  60.2 us (4%)
  other arithmetic  50.7 us (3%)
    psum x7, waiting for transfers between devices, advance(): lax.psum(partial_value.astype(jnp.bfloat16), 'tensor').astype(jnp.float32)  737 us
    all_gather x7, waiting for transfers between devices, advance(): lax.all_gather(normalize(hidden_in, gain_vec), 'tensor', axis=0, tiled=True)  302 us
    all_to_all x7, blocking collectives, advance(): lax.all_to_all(mixed_out, 'tensor', split_axis=1, concat_axis=0, tiled=True)  76.7 us
    unnamed x3, waiting for transfers between devices  45.4 us
    psum x1, waiting for transfers between devices, body(): columns = lax.psum(partial_embed.astype(jnp.bfloat16), 'section')  44.3 us
    all_to_all x7, waiting for transfers between devices, advance(): lax.all_to_all(queries, 'tensor', split_axis=0, concat_axis=1, tiled=True)  37.2 us
    all_to_all x7, starting transfers between devices, advance(): lax.all_to_all(keyvals, 'tensor', split_axis=0, concat_axis=1, tiled=True)  36.6 us
  transfers between devices with their start and end apart: 38, of which 38 were waited for; matrix products, arithmetic and copies ran while one was open for 4% of the time, Pallas kernels for 0%

commit v1 on v0

--- a/solution.py
+++ b/solution.py
@@ -122,7 +122,15 @@
         step_embed = lax.dynamic_index_in_dim(own_embed, step_index, 0, keepdims=False)
         first_input = step_embed.astype(jnp.float32)
         hidden_in = jnp.where(section_pos == 0, first_input, incoming)
-        normed = lax.all_gather(normalize(hidden_in, gain_vec), "tensor", axis=0, tiled=True)
+        normed = jnp.concatenate(
+            lax.all_to_all(
+                jnp.stack([normalize(hidden_in, gain_vec)] * lax.axis_size("tensor")),
+                "tensor",
+                0,
+                0,
+            ),
+            axis=0,
+        )
         queries = jnp.dot(normed, query_mat, preferred_element_type=jnp.float32)
         keyvals = jnp.dot(normed, keyval_mat, preferred_element_type=jnp.float32)
         queries, keyvals = (

time: 1590 us -> 1530 us (0.962)
  waiting for transfers between devices: 1210 us -> 1100 us
  starting transfers between devices: 95.2 us -> 134 us
  matrix products: 77.1 us -> 106 us
    all_gather x7 -> x0, waiting for transfers between devices: 302 us -> none  [advance(): lax.all_gather(normalize(hidden_in, gain_vec), 'tensor', axis=0, tiled=True)]
    all_to_all x0 -> x7, waiting for transfers between devices: none -> 188 us  [advance(): lax.all_to_all(jnp.stack([normalize(hidden_in, gain_vec)] * lax.axis_size...]
    all_to_all x0 -> x7, starting transfers between devices: none -> 39.6 us  [advance(): lax.all_to_all(jnp.stack([normalize(hidden_in, gain_vec)] * lax.axis_size...]
    while x196 -> x77, local copies, waits for them, and re-layouts: 23.7 us -> 5.73 us
  transfers between devices with their start and end apart: 38 -> 38, of which waited for: 38 -> 38; matrix products, arithmetic and copies ran while one was open for 4% -> 5% of each run, Pallas kernels for 0% -> 0%
where the time goes in v1:
time: 1530 us
  waiting for transfers between devices  1100 us (72%)
  starting transfers between devices  134 us (9%)
  matrix products  106 us (7%)
  blocking collectives  76.7 us (5%)
  local copies, waits for them, and re-layouts  64.2 us (4%)
  other arithmetic  35.7 us (2%)
    psum x7, waiting for transfers between devices, advance(): lax.psum(partial_value.astype(jnp.bfloat16), 'tensor').astype(jnp.float32)  742 us
    all_to_all x7, waiting for transfers between devices, advance(): lax.all_to_all(jnp.stack([normalize(hidden_in, gain_vec)] * lax.axis_size...  188 us
    all_to_all x7, blocking collectives, advance(): lax.all_to_all(mixed_out, 'tensor', split_axis=1, concat_axis=0, tiled=True)  76.7 us
    unnamed x3, waiting for transfers between devices  45 us
    psum x1, waiting for transfers between devices, body(): columns = lax.psum(partial_embed.astype(jnp.bfloat16), 'section')  44.3 us
    all_to_all x7, starting transfers between devices, advance(): lax.all_to_all(jnp.stack([normalize(hidden_in, gain_vec)] * lax.axis_size...  39.6 us
    all_to_all x7, waiting for transfers between devices, advance(): lax.all_to_all(queries, 'tensor', split_axis=0, concat_axis=1, tiled=True)  37.6 us
    all_to_all x7, starting transfers between devices, advance(): lax.all_to_all(queries, 'tensor', split_axis=0, concat_axis=1, tiled=True)  36.4 us
  transfers between devices with their start and end apart: 38, of which 38 were waited for; matrix products, arithmetic and copies ran while one was open for 5% of the time, Pallas kernels for 0%

profile of v1, /device:TPU:0, one launch (start us, length us, event | category | flops | bytes accessed | tf_op | source)
XLA Modules:
  0.0 1527.8 jit_solution(15455138357165563362)
XLA Ops:
  8.4 5.9 gather_fusion
  15.4 44.3 %all-reduce.5.cloned.1.call-done = bf16[4,128,256]{2,0,1:T(4,128)(2,1)} async-done(((bf16[4,128,256]{2,0,1:T(4,128)(2,1)}), bf16[4,128,256]{2,0,1:T(4,128)(2,1)}) %all-reduce.5.cloned.1.call-update) | async-done | bytes 262160 | tf_op jit(solution)/shard_map/psum | solution.py:100
  59.7 7.4 all-to-all-start.4
  71.1 4.7 all-to-all-done.4
  76.2 1395.9 %while.19 = (s32[]{:T(128)}, f32[4,8192]{1,0:T(4,128)S(1)}, bf16[4,4,2,1024]{3,1,2,0:T(4,128)(2,1)S(1)}, f32[4,4,8192]{2,1,0:T(4,128)S(1)}, pred[]{:T(512)}, /*i...) while((s32[]{:T(128)}, f32[4,8192]{1,0:T(4,128)S(1)}, ...), condition=%wide.region_8.9_spmd, body=%wide.region_1.8_spmd.sunk | while | flops 1228397952 | bytes 49518836 | solution.py:183
  78.8 4.8 all-to-all-start
  86.7 26.8 %all-to-all-done = bf16[32,4,8192]{2,1,0:T(4,128)(2,1)} async-done(((bf16[32,4,8192]{2,1,0:T(4,128)(2,1)}), bf16[32,4,8192]{2,1,0:T(4,128)(2,1)}, u32[]{:S(2)}, u32[]{:S(2)}) %all-to-all-start) | async-done | bytes 2097184 | tf_op jit(solution)/shard_map/while/body/eval_jaxpr/all_to_all | solution.py:126
  129.0 5.2 all-to-all-start.1
  136.7 5.4 all-to-all-done.1
  146.4 11.0 all_to_all.146
  161.7 104.5 %all-reduce.9.cloned.1.call-done = bf16[128,8192]{1,0:T(8,128)(2,1)} async-done(((bf16[128,8192]{1,0:T(8,128)(2,1)}), bf16[128,8192]{1,0:T(8,128)(2,1)}) %all-reduce.9.cloned.1.call-update) | async-done | bytes 2097168 | tf_op jit(solution)/shard_map/while/body/eval_jaxpr/psum | solution.py:168
  275.8 5.8 all-to-all-start
  284.7 26.9 %all-to-all-done = bf16[32,4,8192]{2,1,0:T(4,128)(2,1)} async-done(((bf16[32,4,8192]{2,1,0:T(4,128)(2,1)}), bf16[32,4,8192]{2,1,0:T(4,128)(2,1)}, u32[]{:S(2)}, u32[]{:S(2)}) %all-to-all-start) | async-done | bytes 2097184 | tf_op jit(solution)/shard_map/while/body/eval_jaxpr/all_to_all | solution.py:126
  327.1 5.2 all-to-all-start.1
  334.7 5.4 all-to-all-done.1
  344.4 11.0 all_to_all.146
  359.7 106.2 %all-reduce.9.cloned.1.call-done = bf16[128,8192]{1,0:T(8,128)(2,1)} async-done(((bf16[128,8192]{1,0:T(8,128)(2,1)}), bf16[128,8192]{1,0:T(8,128)(2,1)}) %all-reduce.9.cloned.1.call-update) | async-done | bytes 2097168 | tf_op jit(solution)/shard_map/while/body/eval_jaxpr/psum | solution.py:168
  475.6 5.8 all-to-all-start
  484.6 26.9 %all-to-all-done = bf16[32,4,8192]{2,1,0:T(4,128)(2,1)} async-done(((bf16[32,4,8192]{2,1,0:T(4,128)(2,1)}), bf16[32,4,8192]{2,1,0:T(4,128)(2,1)}, u32[]{:S(2)}, u32[]{:S(2)}) %all-to-all-start) | async-done | bytes 2097184 | tf_op jit(solution)/shard_map/while/body/eval_jaxpr/all_to_all | solution.py:126
  526.9 5.2 all-to-all-start.1
  534.5 5.4 all-to-all-done.1
  544.3 11.0 all_to_all.146
  559.5 106.2 %all-reduce.9.cloned.1.call-done = bf16[128,8192]{1,0:T(8,128)(2,1)} async-done(((bf16[128,8192]{1,0:T(8,128)(2,1)}), bf16[128,8192]{1,0:T(8,128)(2,1)}) %all-reduce.9.cloned.1.call-update) | async-done | bytes 2097168 | tf_op jit(solution)/shard_map/while/body/eval_jaxpr/psum | solution.py:168
  675.5 5.8 all-to-all-start
  684.4 26.9 %all-to-all-done = bf16[32,4,8192]{2,1,0:T(4,128)(2,1)} async-done(((bf16[32,4,8192]{2,1,0:T(4,128)(2,1)}), bf16[32,4,8192]{2,1,0:T(4,128)(2,1)}, u32[]{:S(2)}, u32[]{:S(2)}) %all-to-all-start) | async-done | bytes 2097184 | tf_op jit(solution)/shard_map/while/body/eval_jaxpr/all_to_all | solution.py:126
  726.7 5.2 all-to-all-start.1
  734.3 5.4 all-to-all-done.1
  744.1 11.0 all_to_all.146
  759.3 106.2 %all-reduce.9.cloned.1.call-done = bf16[128,8192]{1,0:T(8,128)(2,1)} async-done(((bf16[128,8192]{1,0:T(8,128)(2,1)}), bf16[128,8192]{1,0:T(8,128)(2,1)}) %all-reduce.9.cloned.1.call-update) | async-done | bytes 2097168 | tf_op jit(solution)/shard_map/while/body/eval_jaxpr/psum | solution.py:168
  875.3 5.8 all-to-all-start
  884.2 26.9 %all-to-all-done = bf16[32,4,8192]{2,1,0:T(4,128)(2,1)} async-done(((bf16[32,4,8192]{2,1,0:T(4,128)(2,1)}), bf16[32,4,8192]{2,1,0:T(4,128)(2,1)}, u32[]{:S(2)}, u32[]{:S(2)}) %all-to-all-start) | async-done | bytes 2097184 | tf_op jit(solution)/shard_map/while/body/eval_jaxpr/all_to_all | solution.py:126
  926.5 5.2 all-to-all-start.1
  934.1 5.4 all-to-all-done.1
  943.9 11.0 all_to_all.146
  959.1 106.2 %all-reduce.9.cloned.1.call-done = bf16[128,8192]{1,0:T(8,128)(2,1)} async-done(((bf16[128,8192]{1,0:T(8,128)(2,1)}), bf16[128,8192]{1,0:T(8,128)(2,1)}) %all-reduce.9.cloned.1.call-update) | async-done | bytes 2097168 | tf_op jit(solution)/shard_map/while/body/eval_jaxpr/psum | solution.py:168
  1075.1 5.8 all-to-all-start
  1084.0 26.9 %all-to-all-done = bf16[32,4,8192]{2,1,0:T(4,128)(2,1)} async-done(((bf16[32,4,8192]{2,1,0:T(4,128)(2,1)}), bf16[32,4,8192]{2,1,0:T(4,128)(2,1)}, u32[]{:S(2)}, u32[]{:S(2)}) %all-to-all-start) | async-done | bytes 2097184 | tf_op jit(solution)/shard_map/while/body/eval_jaxpr/all_to_all | solution.py:126
  1126.3 5.2 all-to-all-start.1
  1134.0 5.4 all-to-all-done.1
  1143.7 11.0 all_to_all.146
  1158.9 106.2 %all-reduce.9.cloned.1.call-done = bf16[128,8192]{1,0:T(8,128)(2,1)} async-done(((bf16[128,8192]{1,0:T(8,128)(2,1)}), bf16[128,8192]{1,0:T(8,128)(2,1)}) %all-reduce.9.cloned.1.call-update) | async-done | bytes 2097168 | tf_op jit(solution)/shard_map/while/body/eval_jaxpr/psum | solution.py:168
  1274.9 5.8 all-to-all-start
  1283.8 26.9 %all-to-all-done = bf16[32,4,8192]{2,1,0:T(4,128)(2,1)} async-done(((bf16[32,4,8192]{2,1,0:T(4,128)(2,1)}), bf16[32,4,8192]{2,1,0:T(4,128)(2,1)}, u32[]{:S(2)}, u32[]{:S(2)}) %all-to-all-start) | async-done | bytes 2097184 | tf_op jit(solution)/shard_map/while/body/eval_jaxpr/all_to_all | solution.py:126
  1326.1 5.2 all-to-all-start.1
  1333.8 5.4 all-to-all-done.1
  1343.5 11.0 all_to_all.146
  1358.8 106.2 %all-reduce.9.cloned.1.call-done = bf16[128,8192]{1,0:T(8,128)(2,1)} async-done(((bf16[128,8192]{1,0:T(8,128)(2,1)}), bf16[128,8192]{1,0:T(8,128)(2,1)}) %all-reduce.9.cloned.1.call-update) | async-done | bytes 2097168 | tf_op jit(solution)/shard_map/while/body/eval_jaxpr/psum | solution.py:168
  1474.2 44.9 %all-reduce.7.cloned.1.call-done = f32[4,4,8192]{2,1,0:T(4,128)} async-done(((f32[4,4,8192]{2,1,0:T(4,128)}), f32[4,4,8192]{2,1,0:T(4,128)}) %all-reduce.7.cloned.1.call-update) | async-done | bytes 524304
  (460 shorter events, 285.4 us)
Async XLA Ops:
  6.5 60.6 %copy-start.1 = (bf16[1,4,128,2,1024]{4,3,2,1,0:T(2,128)(2,1)S(1)}, bf16[1,4,128,2,1024]{4,3,2,1,0:T(2,128)(2,1)}, u32[]{:S(2)}) copy-start(bf16[1,4,128,2,1024]{4,3,2,1,0:T(2,128)(2,1)} %param.16) | copy-start | bytes 6291460
  6.5 53.1 %all-reduce.5.cloned.1.call-start = ((), (), s32[]{:S(2)}) async-start(), calls=%async_computation.5 | async-start | bytes 524288 | tf_op jit(solution)/shard_map/psum | solution.py:100
  59.7 16.1 %all-to-all-start.4 = ((bf16[4,128,256]{2,0,1:T(4,128)(2,1)}), bf16[4,128,256]{2,0,1:T(4,128)(2,1)S(1)}, u32[]{:S(2)}, u32[]{:S(2)}) async-start(bf16[4,128,256]{2,0,1:T(4,128)(2,1)} %all-reduce.5.cloned.1.call-done), calls=%async_computation.4 | async-start | bytes 524288 | tf_op jit(solution)/shard_map/all_to_all | solution.py:101
  78.8 34.7 %all-to-all-start = ((bf16[32,4,8192]{2,1,0:T(4,128)(2,1)}), bf16[32,4,8192]{2,1,0:T(4,128)(2,1)}, u32[]{:S(2)}, u32[]{:S(2)}) async-start(bf16[32,4,8192]{2,1,0:T(4,128)(2,1)} %stack.25), calls=%async_computation | async-start | bytes 4194304 | tf_op jit(solution)/shard_map/while/body/eval_jaxpr/all_to_all | solution.py:126
  117.8 11.3 all-to-all-start.2
  129.0 13.0 all-to-all-start.1
  134.2 131.9 %all-reduce.9.cloned.1.call-start = ((), (), s32[]{:S(2)}) async-start(), calls=%async_computation.7 | async-start | bytes 4194304 | tf_op jit(solution)/shard_map/while/body/eval_jaxpr/psum | solution.py:168
  161.6 111.6 %copy-start.6 = (s32[4]{0:T(128)S(1)}, s32[4]{0:T(128)}, u32[]{:S(2)}) copy-start(s32[4]{0:T(128)} %get-tuple-element.609) | copy-start | bytes 52 | tf_op jit(solution)/shard_map/while
  267.1 6.1 collective-permute-start
  275.8 35.8 %all-to-all-start = ((bf16[32,4,8192]{2,1,0:T(4,128)(2,1)}), bf16[32,4,8192]{2,1,0:T(4,128)(2,1)}, u32[]{:S(2)}, u32[]{:S(2)}) async-start(bf16[32,4,8192]{2,1,0:T(4,128)(2,1)} %stack.25), calls=%async_computation | async-start | bytes 4194304 | tf_op jit(solution)/shard_map/while/body/eval_jaxpr/all_to_all | solution.py:126
  282.4 51.5 %copy-start.4 = (f32[4,128]{1,0:T(4,128)}, f32[4,128]{1,0:T(4,128)S(1)}, u32[]{:S(2)}) copy-start(f32[4,128]{1,0:T(4,128)S(1)} %get-tuple-element.496) | copy-start | bytes 6148 | tf_op jit(solution)/shard_map/while
  315.8 11.3 all-to-all-start.2
  327.1 13.0 all-to-all-start.1
  332.3 133.7 %all-reduce.9.cloned.1.call-start = ((), (), s32[]{:S(2)}) async-start(), calls=%async_computation.7 | async-start | bytes 4194304 | tf_op jit(solution)/shard_map/while/body/eval_jaxpr/psum | solution.py:168
  359.7 113.4 %copy-start.6 = (s32[4]{0:T(128)S(1)}, s32[4]{0:T(128)}, u32[]{:S(2)}) copy-start(s32[4]{0:T(128)} %get-tuple-element.609) | copy-start | bytes 52 | tf_op jit(solution)/shard_map/while
  466.9 6.1 collective-permute-start
  475.6 35.8 %all-to-all-start = ((bf16[32,4,8192]{2,1,0:T(4,128)(2,1)}), bf16[32,4,8192]{2,1,0:T(4,128)(2,1)}, u32[]{:S(2)}, u32[]{:S(2)}) async-start(bf16[32,4,8192]{2,1,0:T(4,128)(2,1)} %stack.25), calls=%async_computation | async-start | bytes 4194304 | tf_op jit(solution)/shard_map/while/body/eval_jaxpr/all_to_all | solution.py:126
  515.6 11.3 all-to-all-start.2
  526.9 13.0 all-to-all-start.1
  532.1 133.7 %all-reduce.9.cloned.1.call-start = ((), (), s32[]{:S(2)}) async-start(), calls=%async_computation.7 | async-start | bytes 4194304 | tf_op jit(solution)/shard_map/while/body/eval_jaxpr/psum | solution.py:168
  559.5 113.4 %copy-start.6 = (s32[4]{0:T(128)S(1)}, s32[4]{0:T(128)}, u32[]{:S(2)}) copy-start(s32[4]{0:T(128)} %get-tuple-element.609) | copy-start | bytes 52 | tf_op jit(solution)/shard_map/while
  666.7 6.1 collective-permute-start
  675.5 35.8 %all-to-all-start = ((bf16[32,4,8192]{2,1,0:T(4,128)(2,1)}), bf16[32,4,8192]{2,1,0:T(4,128)(2,1)}, u32[]{:S(2)}, u32[]{:S(2)}) async-start(bf16[32,4,8192]{2,1,0:T(4,128)(2,1)} %stack.25), calls=%async_computation | async-start | bytes 4194304 | tf_op jit(solution)/shard_map/while/body/eval_jaxpr/all_to_all | solution.py:126
  682.0 51.5 %copy-start.4 = (f32[4,128]{1,0:T(4,128)}, f32[4,128]{1,0:T(4,128)S(1)}, u32[]{:S(2)}) copy-start(f32[4,128]{1,0:T(4,128)S(1)} %get-tuple-element.496) | copy-start | bytes 6148 | tf_op jit(solution)/shard_map/while
  715.4 11.3 all-to-all-start.2
  726.7 13.0 all-to-all-start.1
  731.9 133.7 %all-reduce.9.cloned.1.call-start = ((), (), s32[]{:S(2)}) async-start(), calls=%async_computation.7 | async-start | bytes 4194304 | tf_op jit(solution)/shard_map/while/body/eval_jaxpr/psum | solution.py:168
  759.3 113.4 %copy-start.6 = (s32[4]{0:T(128)S(1)}, s32[4]{0:T(128)}, u32[]{:S(2)}) copy-start(s32[4]{0:T(128)} %get-tuple-element.609) | copy-start | bytes 52 | tf_op jit(solution)/shard_map/while
  866.5 6.1 collective-permute-start
  875.3 35.8 %all-to-all-start = ((bf16[32,4,8192]{2,1,0:T(4,128)(2,1)}), bf16[32,4,8192]{2,1,0:T(4,128)(2,1)}, u32[]{:S(2)}, u32[]{:S(2)}) async-start(bf16[32,4,8192]{2,1,0:T(4,128)(2,1)} %stack.25), calls=%async_computation | async-start | bytes 4194304 | tf_op jit(solution)/shard_map/while/body/eval_jaxpr/all_to_all | solution.py:126
  915.2 11.3 all-to-all-start.2
  926.5 13.0 all-to-all-start.1
  931.7 133.7 %all-reduce.9.cloned.1.call-start = ((), (), s32[]{:S(2)}) async-start(), calls=%async_computation.7 | async-start | bytes 4194304 | tf_op jit(solution)/shard_map/while/body/eval_jaxpr/psum | solution.py:168
  959.1 113.4 %copy-start.6 = (s32[4]{0:T(128)S(1)}, s32[4]{0:T(128)}, u32[]{:S(2)}) copy-start(s32[4]{0:T(128)} %get-tuple-element.609) | copy-start | bytes 52 | tf_op jit(solution)/shard_map/while
  1066.4 6.1 collective-permute-start
  1075.1 35.8 %all-to-all-start = ((bf16[32,4,8192]{2,1,0:T(4,128)(2,1)}), bf16[32,4,8192]{2,1,0:T(4,128)(2,1)}, u32[]{:S(2)}, u32[]{:S(2)}) async-start(bf16[32,4,8192]{2,1,0:T(4,128)(2,1)} %stack.25), calls=%async_computation | async-start | bytes 4194304 | tf_op jit(solution)/shard_map/while/body/eval_jaxpr/all_to_all | solution.py:126
  1115.1 11.3 all-to-all-start.2
  1126.3 13.0 all-to-all-start.1
  1131.5 133.7 %all-reduce.9.cloned.1.call-start = ((), (), s32[]{:S(2)}) async-start(), calls=%async_computation.7 | async-start | bytes 4194304 | tf_op jit(solution)/shard_map/while/body/eval_jaxpr/psum | solution.py:168
  1158.9 113.4 %copy-start.6 = (s32[4]{0:T(128)S(1)}, s32[4]{0:T(128)}, u32[]{:S(2)}) copy-start(s32[4]{0:T(128)} %get-tuple-element.609) | copy-start | bytes 52 | tf_op jit(solution)/shard_map/while
  1266.2 6.1 collective-permute-start
  1274.9 35.8 %all-to-all-start = ((bf16[32,4,8192]{2,1,0:T(4,128)(2,1)}), bf16[32,4,8192]{2,1,0:T(4,128)(2,1)}, u32[]{:S(2)}, u32[]{:S(2)}) async-start(bf16[32,4,8192]{2,1,0:T(4,128)(2,1)} %stack.25), calls=%async_computation | async-start | bytes 4194304 | tf_op jit(solution)/shard_map/while/body/eval_jaxpr/all_to_all | solution.py:126
  1314.9 11.3 all-to-all-start.2
  1326.1 13.0 all-to-all-start.1
  1331.3 133.7 %all-reduce.9.cloned.1.call-start = ((), (), s32[]{:S(2)}) async-start(), calls=%async_computation.7 | async-start | bytes 4194304 | tf_op jit(solution)/shard_map/while/body/eval_jaxpr/psum | solution.py:168
  1358.7 113.4 %copy-start.6 = (s32[4]{0:T(128)S(1)}, s32[4]{0:T(128)}, u32[]{:S(2)}) copy-start(s32[4]{0:T(128)} %get-tuple-element.609) | copy-start | bytes 52 | tf_op jit(solution)/shard_map/while
  1466.0 6.1 collective-permute-start
  1472.1 47.0 %all-reduce.7.cloned.1.call-start = ((), (), s32[]{:S(2)}) async-start(), calls=%async_computation.6 | async-start | bytes 1048576
  (15 other events, 281.1 us)
Sparse Core Ops, SparseCore 0:
  15.5 44.1 all-reduce.4
  161.8 104.2 all-reduce.8
  359.8 106.0 all-reduce.8
  559.6 106.0 all-reduce.8
  759.4 106.0 all-reduce.8
  959.2 106.0 all-reduce.8
  1159.1 106.0 all-reduce.8
  1358.9 106.0 all-reduce.8
  1475.4 43.6 all-reduce.6
